TPU v7x, 32 devices: a whole 2x2x4 slice. The times are simulated.
32 devices in a mesh: cells: 8 (over z, y), genes: 4 (over x, core).
Axes of the slice: x: 2, y: 2, z: 4, core: 2. Of those that a mesh axis runs over, the one named last changes fastest.
Arguments:
- counts: bfloat16 [1024, 16384], P('cells', 'genes'), may hold values from 0 to 254
- occupancy: int32 [8, 128], P('cells', 'genes'), may hold values 0 or 1
- start_basis: bfloat16 [64, 16384], P(None, 'genes'), may hold values from -0.046875 to 0.046875
Outputs:
- new_basis: float32 [64, 16384], P(None, ('genes', 'cells'))
All inputs are finite; a program needn't handle non-finite values. No bound on the sum of `occupancy` on one device may be relied on, other than what follows from the above.
Results may differ from a plain program's by a relative error of at most 0.01.
Values sent between devices are 32-bit elements; how exact they have to be, the bound alone decides.
No kernel may reach another device: no remote copies, remote signals or barrier semaphores. Data moves between devices by JAX's collectives and lax.ppermute only.
A program may use at most 64 MiB of HBM per device.

v0:
```python
import functools
import math

import jax
import jax.numpy as jnp
from jax import lax
from jax.experimental import pallas as pl
from jax.experimental.pallas import tpu as pltpu
from jax.sharding import PartitionSpec as P

F32 = jnp.float32
BF16 = jnp.bfloat16
NN = (((1,), (0,)), ((), ()))
NT = (((1,), (1,)), ((), ()))
WHOLE = pl.BlockSpec(memory_space=pltpu.VMEM)
SCALARS = pl.BlockSpec(memory_space=pltpu.SMEM)
LANES = 128
PARAMS = pltpu.CompilerParams(vmem_limit_bytes=16 * 2**20)
LOG_PARAMS = pltpu.CompilerParams(vmem_limit_bytes=205 * 2**18)


def dot(a, b, dims):
    return lax.dot_general(a, b, dims, preferred_element_type=F32)


def split_terms(x, count):
    terms = []
    for _ in range(count):
        term = x.astype(BF16)
        terms.append(term)
        x = x - term.astype(F32)
    return terms


def tree_sum(parts):
    while len(parts) > 1:
        parts = [sum(parts[at + 1:at + 2], parts[at]) for at in range(0, len(parts), 2)]
    return parts[0]


def log_kernel(width, counts_hbm, high_ref, low_ref, sum_ref, counts_ref, counts_sem):
    cells, genes = high_ref.shape
    fetches = [
        pltpu.make_async_copy(
            counts_hbm.at[:, pl.ds(at * width, width)], counts_ref.at[:, pl.ds(at * width, width)], counts_sem.at[at]
        )
        for at in range(genes // width)
    ]
    for fetch in fetches:
        fetch.start()
    for at, fetch in enumerate(fetches):
        fetch.wait()
        for begin in range(at * width, (at + 1) * width, LANES):
            lanes = pl.ds(begin, LANES)
            logged = jnp.log(1.0 + counts_ref[:, lanes].astype(F32))
            high = logged.astype(BF16)
            high_ref[:, lanes] = high
            low_ref[:, lanes] = (logged - high.astype(F32)).astype(BF16)
            sum_ref[:, lanes] = jnp.sum(logged, axis=0, keepdims=True)


def log_terms(counts):
    cells, genes = counts.shape
    width = genes // 8
    return pl.pallas_call(
        functools.partial(log_kernel, width),
        out_shape=(
            jax.ShapeDtypeStruct((cells, genes), BF16),
            jax.ShapeDtypeStruct((cells, genes), BF16),
            jax.ShapeDtypeStruct((1, genes), F32),
        ),
        in_specs=[pl.BlockSpec(memory_space=pltpu.HBM)],
        out_specs=(WHOLE, WHOLE, WHOLE),
        scratch_shapes=[pltpu.VMEM(counts.shape, BF16), pltpu.SemaphoreType.DMA((genes // width,))],
        compiler_params=LOG_PARAMS,
        cost_estimate=pl.CostEstimate(flops=20 * cells * genes, bytes_accessed=8 * cells * genes, transcendentals=0),
        name="log_terms",
    )(counts)


def score_kernel(width, occ_ref, basis_ref, high_ref, low_ref, score_ref, lane_ref):
    comps, genes = basis_ref.shape
    edge = genes // occ_ref.shape[1]
    occupancy = occ_ref[...].astype(F32)
    scores = None
    for begin in range(0, genes, width):
        basis = []
        for at in range(begin, begin + width, edge):
            occ = jnp.broadcast_to(occupancy[:, at // edge:at // edge + 1], (1, edge))
            lane_ref[:, pl.ds(at, edge)] = occ
            basis.append(basis_ref[:, pl.ds(at, edge)] * occ.astype(BF16))
        basis = jnp.concatenate(basis, axis=1)
        lanes = pl.ds(begin, width)
        part = dot(basis, high_ref[:, lanes], NT) + dot(basis, low_ref[:, lanes], NT)
        scores = part if scores is None else scores + part
    score_ref[...] = scores


def score_part(occupancy, basis, high, low):
    comps, genes = basis.shape
    cells = high.shape[0]
    return pl.pallas_call(
        functools.partial(score_kernel, genes // 4),
        out_shape=(jax.ShapeDtypeStruct((comps, cells), F32), jax.ShapeDtypeStruct((1, genes), F32)),
        in_specs=[WHOLE] * 4,
        out_specs=(WHOLE, WHOLE),
        compiler_params=PARAMS,
        name="scores",
    )(occupancy, basis, high, low)


def spread_piece(terms, high, low):
    comps = terms[0].shape[0]
    on_low = dot(jnp.concatenate(terms[:2], axis=0), low, NN)
    on_high = dot(jnp.concatenate(terms, axis=0), high, NN)
    small = on_low[comps:] + on_high[2 * comps:]
    middle = on_low[:comps] + on_high[comps:2 * comps]
    return (small + middle) + on_high[:comps]


def spread_kernel(count, picks, me_ref, *refs):
    score_refs, outs = refs[:count], refs[count + 4:]
    high_ref, low_ref, sum_ref, occ_ref = refs[count:count + 4]
    scores = tree_sum([ref[...] for ref in score_refs])
    comps = scores.shape[0]
    terms = split_terms(scores, 3)
    eye = lax.broadcasted_iota(jnp.int32, (comps, LANES), 0) == lax.broadcasted_iota(jnp.int32, (comps, LANES), 1)
    row_sums = jnp.sum(jnp.where(eye, jnp.sum(scores, axis=1, keepdims=True), 0.0), axis=0, keepdims=True)
    chunks = high_ref.shape[1] // (LANES * lax.axis_size("cells"))
    width = chunks * LANES
    for pick, out in zip(picks, outs):
        start = pl.multiple_of((me_ref[0] ^ pick) * width, width)
        lanes = pl.ds(start, width)
        piece = spread_piece(terms, high_ref[:, lanes], low_ref[:, lanes]) * occ_ref[:, lanes]
        sums = sum_ref[:, lanes] * occ_ref[:, lanes]
        extra = [row_sums]
        for at in range(chunks):
            out[at * comps:(at + 1) * comps] = piece[:, at * LANES:(at + 1) * LANES]
            extra.append(sums[:, at * LANES:(at + 1) * LANES])
        extra.append(jnp.zeros((out.shape[0] - chunks * comps - chunks - 1, LANES), F32))
        out[chunks * comps:] = jnp.concatenate(extra, axis=0)


def block_rows(comps, chunks):
    return comps * chunks + -(-(chunks + 1) // 8) * 8


def spread_pieces(me, scores, high, low, sums, occ, picks):
    comps = scores[0].shape[0]
    chunks = high.shape[1] // (LANES * lax.axis_size("cells"))
    block = jax.ShapeDtypeStruct((block_rows(comps, chunks), LANES), F32)
    return pl.pallas_call(
        functools.partial(spread_kernel, len(scores), picks),
        out_shape=[block] * len(picks),
        in_specs=[SCALARS] + [WHOLE] * (len(scores) + 4),
        out_specs=[WHOLE] * len(picks),
        compiler_params=PARAMS,
        cost_estimate=pl.CostEstimate(
            flops=10 * comps * len(picks) * chunks * LANES * high.shape[0], bytes_accessed=2**21, transcendentals=0
        ),
        name="spread",
    )(me, *scores, high, low, sums, occ)


def gram_kernel(scale, chunks, *refs):
    pieces, (spread_ref, gram_ref) = refs[:-2], refs[-2:]
    comps = spread_ref.shape[0]
    total = tree_sum([ref[...] for ref in pieces])
    extra = total[chunks * comps:chunks * comps + chunks + 1]
    eye = lax.broadcasted_iota(jnp.int32, (comps, LANES), 0) == lax.broadcasted_iota(jnp.int32, (comps, LANES), 1)
    row_sums = jnp.sum(jnp.where(eye, extra[:1], 0.0), axis=1, keepdims=True) * scale
    parts = [total[at * comps:(at + 1) * comps] - row_sums * extra[at + 1:at + 2] for at in range(chunks)]
    spread = jnp.concatenate(parts, axis=1)
    spread_ref[...] = spread
    gram_ref[...] = packed_gram(spread)


def packed_gram(spread):
    gram = lax.dot_general(spread, spread, NT, precision=lax.Precision.HIGHEST, preferred_element_type=F32)
    half = spread.shape[0] // 2
    return jnp.concatenate([gram[:half], gram[half:]], axis=1)


def centered_gram(pieces, comps, cell_total):
    chunks = pieces[0].shape[0] // comps
    return pl.pallas_call(
        functools.partial(gram_kernel, 1.0 / cell_total, chunks),
        out_shape=(
            jax.ShapeDtypeStruct((comps, chunks * LANES), F32),
            jax.ShapeDtypeStruct((comps // 2, comps * 2), F32),
        ),
        in_specs=[WHOLE] * len(pieces),
        out_specs=(WHOLE, WHOLE),
        compiler_params=PARAMS,
        name="gram",
    )(*pieces)


def plain_gram_kernel(scale, spread_ref, row_ref, sum_ref, out_ref, gram_ref):
    spread = spread_ref[...] - row_ref[...] * scale * sum_ref[...]
    out_ref[...] = spread
    gram_ref[...] = packed_gram(spread)


def plain_gram(spread, rows, sums, cell_total):
    comps, width = spread.shape
    return pl.pallas_call(
        functools.partial(plain_gram_kernel, 1.0 / cell_total),
        out_shape=(
            jax.ShapeDtypeStruct((comps, width), F32),
            jax.ShapeDtypeStruct((comps // 2, comps * 2), F32),
        ),
        in_specs=[WHOLE] * 3,
        out_specs=(WHOLE, WHOLE),
        compiler_params=PARAMS,
        name="plain_gram",
    )(spread, rows, sums)


def inverse_of(x):
    guess = pl.reciprocal(x, approx=True)
    for _ in range(2):
        guess = guess * (2.0 - x * guess)
    return guess


def row_of(x, at):
    return jnp.broadcast_to(x[at:at + 1, :], x.shape)


def eliminate(groups, edge):
    groups = list(groups)
    below = lax.broadcasted_iota(jnp.int32, groups[0].shape, 0)
    for at in range(len(groups)):
        spread = [
            [jnp.broadcast_to(rows[:, c:c + 1], rows.shape) for c in range(at * edge, (at + 1) * edge)]
            for rows in groups[at:]
        ]
        for i in range(0, edge, 2):
            cols = spread[0]
            first, second = cols[i], cols[i + 1]
            a, b, c = row_of(first, i), row_of(second, i), row_of(second, i + 1)
            inv_a = inverse_of(a)
            inv_c = a * inverse_of(a * c - b * b)
            ratio = b * inv_a
            factors = []
            for k in range(i + 2, edge):
                top = row_of(cols[k], i)
                factors.append((k, top * inv_a, (row_of(cols[k], i + 1) - ratio * top) * inv_c))
            rows = groups[at]
            upper = row_of(rows, i) * inv_a
            rows = rows - jnp.where(below > i, first, 0.0) * upper
            lower = row_of(rows, i + 1) * inv_c
            groups[at] = rows - jnp.where(below > i + 1, second - ratio * first, 0.0) * lower
            for ahead, cols in enumerate(spread):
                first = cols[i]
                second = cols[i + 1] - ratio * first
                for k, on_first, on_second in factors:
                    cols[k] = cols[k] - first * on_first - second * on_second
                if ahead:
                    groups[at + ahead] = groups[at + ahead] - first * upper - second * lower
    return groups


def basis_kernel(scale, *refs):
    grams, (spread_ref, out_ref) = refs[:-2], refs[-2:]
    gram = tree_sum([ref[...] for ref in grams])
    comps = spread_ref.shape[0]
    gram = jnp.concatenate([gram[:, :comps], gram[:, comps:]], axis=0)
    row_at = lax.broadcasted_iota(jnp.int32, (comps, comps), 0)
    col_at = lax.broadcasted_iota(jnp.int32, (comps, comps), 1)
    eye = row_at == col_at
    trace = jnp.sum(jnp.where(eye, gram, 0.0), axis=(0, 1), keepdims=True)
    both = jnp.concatenate([gram * (1.0 / trace), jnp.where(eye, 1.0, 0.0).astype(F32)], axis=1)
    groups = eliminate([both[at:at + 8] for at in range(0, comps, 8)], 8)
    both = jnp.concatenate(groups, axis=0)
    pivots = jnp.sum(jnp.where(eye, both[:, :comps], 0.0), axis=1, keepdims=True)
    inverse = both[:, comps:] * (scale / jnp.sqrt(pivots) / jnp.sqrt(trace))
    out_ref[...] = lax.dot_general(
        inverse, spread_ref[...], NN, precision=lax.Precision.HIGHEST, preferred_element_type=F32
    )


def orthonormal(grams, spread, scale):
    return pl.pallas_call(
        functools.partial(basis_kernel, scale),
        out_shape=jax.ShapeDtypeStruct(spread.shape, F32),
        in_specs=[WHOLE] * (len(grams) + 1),
        out_specs=WHOLE,
        compiler_params=PARAMS,
        name="orthonormal",
    )(*grams, spread)


def send(x, offset_cells, offset_genes):
    cells, genes = lax.axis_size("cells"), lax.axis_size("genes")
    pairs = []
    for c in range(cells):
        for g in range(genes):
            pairs.append((c * genes + g, (c ^ offset_cells) * genes + (g ^ offset_genes)))
    return lax.ppermute(x, ("cells", "genes"), pairs)


def gene_terms(x):
    terms = [x, send(x, 0, 1)]
    for at in range(1, lax.axis_size("genes").bit_length() - 1):
        x = tree_sum(terms)
        terms = [x, send(x, 0, 1 << at | 1)]
    return terms


def cell_terms(x):
    terms = [x]
    for at in range(lax.axis_size("cells").bit_length() - 1):
        x = tree_sum(terms)
        terms = [x, send(x, 1 << at, 1)]
    return terms


def scattered_spread(scores, high, low, sums, occ, cell_total):
    comps = scores[0].shape[0]
    me = lax.axis_index("cells").astype(jnp.int32).reshape(1)
    make = functools.partial(spread_pieces, scores=scores, high=high, low=low, sums=sums, occ=occ)
    blocks = list(make(me, picks=[7, 6, 5]))
    blocks[0], me = lax.optimization_barrier((blocks[0], me))
    came = [send(x, k - 4, 1) for k, x in zip((7, 6, 5), blocks)]
    far, near, own, *blocks = make(me, picks=[4, 2, 0, 3, 1])
    far, near = send(far, 0, 1), send(near, 0, 1)
    near = send(near + send(blocks[0], 1, 1), 2, 1)
    also = send(blocks[1], 1, 0)
    far = send(far + lax.optimization_barrier(tree_sum(came)), 4, 1)
    return centered_gram([own + also + (near + far)], comps, cell_total)


def all_alike(counts, occupancy, start_basis):
    tile_rows, tile_cols = occupancy.shape
    edge = counts.shape[0] // tile_rows
    logged = jnp.log(1.0 + counts.astype(F32)).reshape(tile_rows, edge, tile_cols, -1)
    logged = (logged * occupancy.astype(F32)[:, None, :, None]).reshape(counts.shape)
    high, low = split_terms(logged, 2)
    scores = lax.psum(dot(start_basis, high, NT) + dot(start_basis, low, NT), "genes")
    spread = spread_piece(split_terms(scores, 3), high, low)
    spread = lax.psum_scatter(spread, "cells", scatter_dimension=1, tiled=True)
    rows = lax.psum(jnp.sum(scores, axis=1, keepdims=True), "cells")
    sums = lax.psum_scatter(jnp.sum(logged, axis=0, keepdims=True), "cells", scatter_dimension=1, tiled=True)
    spread, gram = plain_gram(spread, rows, sums, counts.shape[0] * lax.axis_size("cells"))
    return [lax.psum(gram, ("cells", "genes"))], spread


def in_steps(counts, occupancy, start_basis):
    high, low, sums = log_terms(counts)
    scores, occ = score_part(occupancy, start_basis, high, low)
    cell_total = counts.shape[0] * lax.axis_size("cells")
    spread, gram = scattered_spread(gene_terms(scores), high, low, sums, occ, cell_total)
    return cell_terms(tree_sum(gene_terms(gram))), spread


def on_device(counts, occupancy, start_basis):
    gene_count = counts.shape[1]
    cells, genes = lax.axis_size("cells"), lax.axis_size("genes")
    halvings = cells == 1 << 3 and genes == 1 << 2
    tiles = occupancy.shape[0] == 1 and gene_count == occupancy.shape[1] * LANES
    work = in_steps if halvings and tiles and gene_count % (cells * LANES) == 0 else all_alike
    grams, spread = work(counts, occupancy, start_basis)
    return orthonormal(grams, spread, math.sqrt(gene_count * genes))


def solution(mesh):
    in_specs = (P("cells", "genes"), P("cells", "genes"), P(None, "genes"))
    out_specs = P(None, ("genes", "cells"))
    return jax.shard_map(
        on_device, mesh=mesh, in_specs=in_specs, out_specs=out_specs, check_vma=False
    )
```

profile of v0, /device:TPU:0, one launch (start us, length us, event | category | flops | bytes accessed | tf_op | source)
XLA Modules:
  0.0 48.5 jit_solution(18317924303643290599)
XLA Ops:
  0.0 1.9 %log_terms.1 = (bf16[128,4096]{1,0:T(8,128)(2,1)S(1)}, bf16[128,4096]{1,0:T(8,128)(2,1)S(1)}, f32[1,4096]{1,0:T(1,128)S(1)}) custom-call(bf16[128,4096]{1,0:T(8,128)(2,1)} %counts_hbm.1), custom_call_target="tpu_custom_call" | custom-call | flops 10485760 | bytes 4194304 | tf_op jit(solution)/shard_map/log_terms/pallas_call | solution.py:65
  1.9 0.6 %copy-done.1 = s32[1,32]{1,0:T(1,128)S(1)} copy-done((s32[1,32]{1,0:T(1,128)S(1)}, s32[1,32]{1,0:T(1,128)}, u32[]{:S(2)}) %copy-start.1) | copy-done | bytes 152
  2.6 0.9 %scores.1 = (f32[64,128]{1,0:T(8,128)S(1)}, f32[1,4096]{1,0:T(1,128)S(1)}) custom-call(s32[1,32]{1,0:T(1,128)S(1)} %copy-done.1, bf16[64,4096]{1,0:T(8,128)(2,1)S(1)} %copy-done, bf16[128,4096]{1,0:T(8,128)(2,1)S(1)} %get-tuple-element.22.high_ref.refs_2_, bf16[128,4096]{1,0:T(8,128)(2,1)S(1)} %get-tuple-element.23.low_ref.refs_3_), custom_call_target="tpu_custom_call" | custom-call | tf_op jit(solution)/shard_map/scores/pallas_call | solution.py:102
  4.0 0.9 %collective-permute-done = f32[64,128]{1,0:T(8,128)S(1)} collective-permute-done((f32[64,128]{1,0:T(8,128)S(1)}, f32[64,128]{1,0:T(8,128)S(1)}, u32[]{:S(2)}, u32[]{:S(2)}) %collective-permute-start) | collective-permute-done | bytes 32800 | tf_op jit(solution)/shard_map/ppermute | solution.py:301
  4.8 2.6 %collective-permute-start.1 = (f32[64,128]{1,0:T(8,128)S(1)}, f32[64,128]{1,0:T(8,128)S(1)}, u32[]{:S(2)}, u32[]{:S(2)}) collective-permute-start(f32[64,128]{1,0:T(8,128)S(1)} %add.36.refs_0_), channel_id=1, source_target_pairs={{0,3},{1,2},{2,1},{3,0},{4,7},{5,6},{6,5},{7,4},{8,11},{9,10},{10,... | collective-permute-start | bytes 98312 | tf_op jit(solution)/shard_map/ppermute | solution.py:301
  7.5 1.6 %collective-permute-done.1.refs_1_ = f32[64,128]{1,0:T(8,128)S(1)} collective-permute-done((f32[64,128]{1,0:T(8,128)S(1)}, f32[64,128]{1,0:T(8,128)S(1)}, u32[]{:S(2)}, u32[]{:S(2)}) %collective-permute-start.1) | collective-permute-done | bytes 32800 | tf_op jit(solution)/shard_map/ppermute | solution.py:301
  9.5 2.9 %collective-permute-start.7 = (f32[264,128]{1,0:T(8,128)S(1)}, f32[264,128]{1,0:T(8,128)S(1)}, u32[]{:S(2)}, u32[]{:S(2)}) collective-permute-start(f32[264,128]{1,0:T(8,128)S(1)} %get-tuple-element.34), channel_id=1, source_target_pairs={{0,13},{1,12},{2,15},{3,14},{4,9},{5,8},{6,11},{7,10},{8,5},{9,4},... | collective-permute-start | bytes 405512 | tf_op jit(solution)/shard_map/ppermute | solution.py:301
  14.1 2.2 %collective-permute-done.7 = f32[264,128]{1,0:T(8,128)S(1)} collective-permute-done((f32[264,128]{1,0:T(8,128)S(1)}, f32[264,128]{1,0:T(8,128)S(1)}, u32[]{:S(2)}, u32[]{:S(2)}) %collective-permute-start.7) | collective-permute-done | bytes 135200 | tf_op jit(solution)/shard_map/ppermute | solution.py:301
  16.2 1.8 %collective-permute-start.4 = (f32[264,128]{1,0:T(8,128)S(1)}, f32[264,128]{1,0:T(8,128)S(1)}, u32[]{:S(2)}, u32[]{:S(2)}) collective-permute-start(f32[264,128]{1,0:T(8,128)S(1)} %get-tuple-element.32), channel_id=1, source_target_pairs={{0,5},{1,4},{2,7},{3,6},{4,1},{5,0},{6,3},{7,2},{8,13},{9,12},{10,... | collective-permute-start | bytes 405512 | tf_op jit(solution)/shard_map/ppermute | solution.py:301
  18.0 1.5 %collective-permute-done.8 = f32[264,128]{1,0:T(8,128)S(1)} collective-permute-done((f32[264,128]{1,0:T(8,128)S(1)}, f32[264,128]{1,0:T(8,128)S(1)}, u32[]{:S(2)}, u32[]{:S(2)}) %collective-permute-start.8) | collective-permute-done | bytes 135200 | tf_op jit(solution)/shard_map/ppermute | solution.py:301
  19.6 2.8 %collective-permute-start.10 = (f32[264,128]{1,0:T(8,128)S(1)}, f32[264,128]{1,0:T(8,128)S(1)}, u32[]{:S(2)}, u32[]{:S(2)}) collective-permute-start(f32[264,128]{1,0:T(8,128)S(1)} %add.41), channel_id=1, source_target_pairs={{0,17},{1,16},{2,19},{3,18},{4,21},{5,20},{6,23},{7,22},{8,25},{9,... | collective-permute-start | bytes 405512 | tf_op jit(solution)/shard_map/ppermute | solution.py:301
  22.5 1.6 %collective-permute-start.5 = (f32[264,128]{1,0:T(8,128)S(1)}, f32[264,128]{1,0:T(8,128)S(1)}, u32[]{:S(2)}, u32[]{:S(2)}) collective-permute-start(f32[264,128]{1,0:T(8,128)S(1)} %add.38), channel_id=1, source_target_pairs={{0,9},{1,8},{2,11},{3,10},{4,13},{5,12},{6,15},{7,14},{8,1},{9,0},... | collective-permute-start | bytes 405512 | tf_op jit(solution)/shard_map/ppermute | solution.py:301
  24.0 1.4 %collective-permute-done.2 = f32[264,128]{1,0:T(8,128)S(1)} collective-permute-done((f32[264,128]{1,0:T(8,128)S(1)}, f32[264,128]{1,0:T(8,128)S(1)}, u32[]{:S(2)}, u32[]{:S(2)}) %collective-permute-start.2) | collective-permute-done | bytes 135200 | tf_op jit(solution)/shard_map/ppermute | solution.py:301
  25.4 3.7 %collective-permute-done.10 = f32[264,128]{1,0:T(8,128)S(1)} collective-permute-done((f32[264,128]{1,0:T(8,128)S(1)}, f32[264,128]{1,0:T(8,128)S(1)}, u32[]{:S(2)}, u32[]{:S(2)}) %collective-permute-start.10) | collective-permute-done | bytes 135200 | tf_op jit(solution)/shard_map/ppermute | solution.py:301
  30.1 0.8 %collective-permute-done.11 = f32[32,128]{1,0:T(8,128)S(1)} collective-permute-done((f32[32,128]{1,0:T(8,128)S(1)}, f32[32,128]{1,0:T(8,128)S(1)}, u32[]{:S(2)}, u32[]{:S(2)}) %collective-permute-start.11) | collective-permute-done | bytes 16416 | tf_op jit(solution)/shard_map/ppermute | solution.py:301
  30.9 1.8 %collective-permute-start.12 = (f32[32,128]{1,0:T(8,128)S(1)}, f32[32,128]{1,0:T(8,128)S(1)}, u32[]{:S(2)}, u32[]{:S(2)}) collective-permute-start(f32[32,128]{1,0:T(8,128)S(1)} %add.44), channel_id=1, source_target_pairs={{0,3},{1,2},{2,1},{3,0},{4,7},{5,6},{6,5},{7,4},{8,11},{9,10},{10,... | collective-permute-start | bytes 49160 | tf_op jit(solution)/shard_map/ppermute | solution.py:301
  32.8 1.4 %collective-permute-done.12 = f32[32,128]{1,0:T(8,128)S(1)} collective-permute-done((f32[32,128]{1,0:T(8,128)S(1)}, f32[32,128]{1,0:T(8,128)S(1)}, u32[]{:S(2)}, u32[]{:S(2)}) %collective-permute-start.12) | collective-permute-done | bytes 16416 | tf_op jit(solution)/shard_map/ppermute | solution.py:301
  34.2 1.8 %collective-permute-start.13 = (f32[32,128]{1,0:T(8,128)S(1)}, f32[32,128]{1,0:T(8,128)S(1)}, u32[]{:S(2)}, u32[]{:S(2)}) collective-permute-start(f32[32,128]{1,0:T(8,128)S(1)} %add.45), channel_id=1, source_target_pairs={{0,5},{1,4},{2,7},{3,6},{4,1},{5,0},{6,3},{7,2},{8,13},{9,12},{10,... | collective-permute-start | bytes 49160 | tf_op jit(solution)/shard_map/ppermute | solution.py:301
  36.0 1.4 %collective-permute-done.13 = f32[32,128]{1,0:T(8,128)S(1)} collective-permute-done((f32[32,128]{1,0:T(8,128)S(1)}, f32[32,128]{1,0:T(8,128)S(1)}, u32[]{:S(2)}, u32[]{:S(2)}) %collective-permute-start.13) | collective-permute-done | bytes 16416 | tf_op jit(solution)/shard_map/ppermute | solution.py:301
  37.4 1.5 %collective-permute-start.14 = (f32[32,128]{1,0:T(8,128)S(1)}, f32[32,128]{1,0:T(8,128)S(1)}, u32[]{:S(2)}, u32[]{:S(2)}) collective-permute-start(f32[32,128]{1,0:T(8,128)S(1)} %add.46), channel_id=1, source_target_pairs={{0,9},{1,8},{2,11},{3,10},{4,13},{5,12},{6,15},{7,14},{8,1},{9,0},... | collective-permute-start | bytes 49160 | tf_op jit(solution)/shard_map/ppermute | solution.py:301
  39.0 1.6 %collective-permute-done.14 = f32[32,128]{1,0:T(8,128)S(1)} collective-permute-done((f32[32,128]{1,0:T(8,128)S(1)}, f32[32,128]{1,0:T(8,128)S(1)}, u32[]{:S(2)}, u32[]{:S(2)}) %collective-permute-start.14) | collective-permute-done | bytes 16416 | tf_op jit(solution)/shard_map/ppermute | solution.py:301
  40.6 3.2 %collective-permute-start.15 = (f32[32,128]{1,0:T(8,128)S(1)}, f32[32,128]{1,0:T(8,128)S(1)}, u32[]{:S(2)}, u32[]{:S(2)}) collective-permute-start(f32[32,128]{1,0:T(8,128)S(1)} %add.47.refs_0_), channel_id=1, source_target_pairs={{0,17},{1,16},{2,19},{3,18},{4,21},{5,20},{6,23},{7,22},{8,25},{9,... | collective-permute-start | bytes 49160 | tf_op jit(solution)/shard_map/ppermute | solution.py:301
  43.8 1.4 %collective-permute-done.15.refs_1_ = f32[32,128]{1,0:T(8,128)S(1)} collective-permute-done((f32[32,128]{1,0:T(8,128)S(1)}, f32[32,128]{1,0:T(8,128)S(1)}, u32[]{:S(2)}, u32[]{:S(2)}) %collective-permute-start.15) | collective-permute-done | bytes 16416 | tf_op jit(solution)/shard_map/ppermute | solution.py:301
  45.3 3.2 %orthonormal.1 = f32[64,512]{1,0:T(8,128)} custom-call(f32[32,128]{1,0:T(8,128)S(1)} %add.47.refs_0_, f32[32,128]{1,0:T(8,128)S(1)} %collective-permute-done.15.refs_1_, f32[64,512]{1,0:T(8,128)S(1)} %get-tuple-element.38.refs_2_), custom_call_target="tpu_custom_call" | custom-call | tf_op jit(solution)/shard_map/orthonormal/pallas_call | solution.py:285
  (27 shorter events, 3.7 us)
Async XLA Ops:
  0.0 1.9 %copy-start = (bf16[64,4096]{1,0:T(8,128)(2,1)S(1)}, bf16[64,4096]{1,0:T(8,128)(2,1)}, u32[]{:S(2)}) copy-start(bf16[64,4096]{1,0:T(8,128)(2,1)} %basis_ref.1) | copy-start | bytes 1572868
  1.9 0.7 %copy-start.1 = (s32[1,32]{1,0:T(1,128)S(1)}, s32[1,32]{1,0:T(1,128)}, u32[]{:S(2)}) copy-start(s32[1,32]{1,0:T(1,128)} %occ_ref.1) | copy-start | bytes 388
  3.5 1.4 %collective-permute-start = (f32[64,128]{1,0:T(8,128)S(1)}, f32[64,128]{1,0:T(8,128)S(1)}, u32[]{:S(2)}, u32[]{:S(2)}) collective-permute-start(f32[64,128]{1,0:T(8,128)S(1)} %get-tuple-element.24), channel_id=1, source_target_pairs={{0,1},{1,0},{2,3},{3,2},{4,5},{5,4},{6,7},{7,6},{8,9},{9,8},{10,11... | collective-permute-start | bytes 98312 | tf_op jit(solution)/shard_map/ppermute | solution.py:301
  4.8 4.2 %collective-permute-start.1 = (f32[64,128]{1,0:T(8,128)S(1)}, f32[64,128]{1,0:T(8,128)S(1)}, u32[]{:S(2)}, u32[]{:S(2)}) collective-permute-start(f32[64,128]{1,0:T(8,128)S(1)} %add.36.refs_0_), channel_id=1, source_target_pairs={{0,3},{1,2},{2,1},{3,0},{4,7},{5,6},{6,5},{7,4},{8,11},{9,10},{10,... | collective-permute-start | bytes 98312 | tf_op jit(solution)/shard_map/ppermute | solution.py:301
  9.5 6.8 %collective-permute-start.7 = (f32[264,128]{1,0:T(8,128)S(1)}, f32[264,128]{1,0:T(8,128)S(1)}, u32[]{:S(2)}, u32[]{:S(2)}) collective-permute-start(f32[264,128]{1,0:T(8,128)S(1)} %get-tuple-element.34), channel_id=1, source_target_pairs={{0,13},{1,12},{2,15},{3,14},{4,9},{5,8},{6,11},{7,10},{8,5},{9,4},... | collective-permute-start | bytes 405512 | tf_op jit(solution)/shard_map/ppermute | solution.py:301
  12.3 7.2 %collective-permute-start.8 = (f32[264,128]{1,0:T(8,128)S(1)}, f32[264,128]{1,0:T(8,128)S(1)}, u32[]{:S(2)}, u32[]{:S(2)}) collective-permute-start(f32[264,128]{1,0:T(8,128)S(1)} %get-tuple-element.35), channel_id=1, source_target_pairs={{0,9},{1,8},{2,11},{3,10},{4,13},{5,12},{6,15},{7,14},{8,1},{9,0},... | collective-permute-start | bytes 405512 | tf_op jit(solution)/shard_map/ppermute | solution.py:301
  12.7 6.8 %collective-permute-start.9 = (f32[264,128]{1,0:T(8,128)S(1)}, f32[264,128]{1,0:T(8,128)S(1)}, u32[]{:S(2)}, u32[]{:S(2)}) collective-permute-start(f32[264,128]{1,0:T(8,128)S(1)} %get-tuple-element.36), channel_id=1, source_target_pairs={{0,5},{1,4},{2,7},{3,6},{4,1},{5,0},{6,3},{7,2},{8,13},{9,12},{10,... | collective-permute-start | bytes 405512 | tf_op jit(solution)/shard_map/ppermute | solution.py:301
  13.5 6.1 %collective-permute-start.6 = (f32[264,128]{1,0:T(8,128)S(1)}, f32[264,128]{1,0:T(8,128)S(1)}, u32[]{:S(2)}, u32[]{:S(2)}) collective-permute-start(f32[264,128]{1,0:T(8,128)S(1)} %get-tuple-element.33), channel_id=1, source_target_pairs={{0,1},{1,0},{2,3},{3,2},{4,5},{5,4},{6,7},{7,6},{8,9},{9,8},{10,11... | collective-permute-start | bytes 405512 | tf_op jit(solution)/shard_map/ppermute | solution.py:301
  13.7 8.7 %collective-permute-start.3 = (f32[264,128]{1,0:T(8,128)S(1)}, f32[264,128]{1,0:T(8,128)S(1)}, u32[]{:S(2)}, u32[]{:S(2)}) collective-permute-start(f32[264,128]{1,0:T(8,128)S(1)} %get-tuple-element.31), channel_id=1, source_target_pairs={{0,1},{1,0},{2,3},{3,2},{4,5},{5,4},{6,7},{7,6},{8,9},{9,8},{10,11... | collective-permute-start | bytes 405512 | tf_op jit(solution)/shard_map/ppermute | solution.py:301
  16.2 6.2 %collective-permute-start.4 = (f32[264,128]{1,0:T(8,128)S(1)}, f32[264,128]{1,0:T(8,128)S(1)}, u32[]{:S(2)}, u32[]{:S(2)}) collective-permute-start(f32[264,128]{1,0:T(8,128)S(1)} %get-tuple-element.32), channel_id=1, source_target_pairs={{0,5},{1,4},{2,7},{3,6},{4,1},{5,0},{6,3},{7,2},{8,13},{9,12},{10,... | collective-permute-start | bytes 405512 | tf_op jit(solution)/shard_map/ppermute | solution.py:301
  19.5 5.9 %collective-permute-start.2 = (f32[264,128]{1,0:T(8,128)S(1)}, f32[264,128]{1,0:T(8,128)S(1)}, u32[]{:S(2)}, u32[]{:S(2)}) collective-permute-start(f32[264,128]{1,0:T(8,128)S(1)} %get-tuple-element.30), channel_id=1, source_target_pairs={{0,4},{1,5},{2,6},{3,7},{4,0},{5,1},{6,2},{7,3},{8,12},{9,13},{10,... | collective-permute-start | bytes 405512 | tf_op jit(solution)/shard_map/ppermute | solution.py:301
  19.6 9.5 %collective-permute-start.10 = (f32[264,128]{1,0:T(8,128)S(1)}, f32[264,128]{1,0:T(8,128)S(1)}, u32[]{:S(2)}, u32[]{:S(2)}) collective-permute-start(f32[264,128]{1,0:T(8,128)S(1)} %add.41), channel_id=1, source_target_pairs={{0,17},{1,16},{2,19},{3,18},{4,21},{5,20},{6,23},{7,22},{8,25},{9,... | collective-permute-start | bytes 405512 | tf_op jit(solution)/shard_map/ppermute | solution.py:301
  22.5 6.7 %collective-permute-start.5 = (f32[264,128]{1,0:T(8,128)S(1)}, f32[264,128]{1,0:T(8,128)S(1)}, u32[]{:S(2)}, u32[]{:S(2)}) collective-permute-start(f32[264,128]{1,0:T(8,128)S(1)} %add.38), channel_id=1, source_target_pairs={{0,9},{1,8},{2,11},{3,10},{4,13},{5,12},{6,15},{7,14},{8,1},{9,0},... | collective-permute-start | bytes 405512 | tf_op jit(solution)/shard_map/ppermute | solution.py:301
  29.6 1.4 %collective-permute-start.11 = (f32[32,128]{1,0:T(8,128)S(1)}, f32[32,128]{1,0:T(8,128)S(1)}, u32[]{:S(2)}, u32[]{:S(2)}) collective-permute-start(f32[32,128]{1,0:T(8,128)S(1)} %get-tuple-element.37), channel_id=1, source_target_pairs={{0,1},{1,0},{2,3},{3,2},{4,5},{5,4},{6,7},{7,6},{8,9},{9,8},{10,11... | collective-permute-start | bytes 49160 | tf_op jit(solution)/shard_map/ppermute | solution.py:301
  30.9 3.3 %collective-permute-start.12 = (f32[32,128]{1,0:T(8,128)S(1)}, f32[32,128]{1,0:T(8,128)S(1)}, u32[]{:S(2)}, u32[]{:S(2)}) collective-permute-start(f32[32,128]{1,0:T(8,128)S(1)} %add.44), channel_id=1, source_target_pairs={{0,3},{1,2},{2,1},{3,0},{4,7},{5,6},{6,5},{7,4},{8,11},{9,10},{10,... | collective-permute-start | bytes 49160 | tf_op jit(solution)/shard_map/ppermute | solution.py:301
  34.2 3.2 %collective-permute-start.13 = (f32[32,128]{1,0:T(8,128)S(1)}, f32[32,128]{1,0:T(8,128)S(1)}, u32[]{:S(2)}, u32[]{:S(2)}) collective-permute-start(f32[32,128]{1,0:T(8,128)S(1)} %add.45), channel_id=1, source_target_pairs={{0,5},{1,4},{2,7},{3,6},{4,1},{5,0},{6,3},{7,2},{8,13},{9,12},{10,... | collective-permute-start | bytes 49160 | tf_op jit(solution)/shard_map/ppermute | solution.py:301
  37.4 3.2 %collective-permute-start.14 = (f32[32,128]{1,0:T(8,128)S(1)}, f32[32,128]{1,0:T(8,128)S(1)}, u32[]{:S(2)}, u32[]{:S(2)}) collective-permute-start(f32[32,128]{1,0:T(8,128)S(1)} %add.46), channel_id=1, source_target_pairs={{0,9},{1,8},{2,11},{3,10},{4,13},{5,12},{6,15},{7,14},{8,1},{9,0},... | collective-permute-start | bytes 49160 | tf_op jit(solution)/shard_map/ppermute | solution.py:301
  40.6 4.7 %collective-permute-start.15 = (f32[32,128]{1,0:T(8,128)S(1)}, f32[32,128]{1,0:T(8,128)S(1)}, u32[]{:S(2)}, u32[]{:S(2)}) collective-permute-start(f32[32,128]{1,0:T(8,128)S(1)} %add.47.refs_0_), channel_id=1, source_target_pairs={{0,17},{1,16},{2,19},{3,18},{4,21},{5,20},{6,23},{7,22},{8,25},{9,... | collective-permute-start | bytes 49160 | tf_op jit(solution)/shard_map/ppermute | solution.py:301
where the time goes:
time: 48.7 us; the launch traced here: 48.5 us
  starting transfers between devices  22.2 us (46%)
  waiting for transfers between devices  18.1 us (37%)
  Pallas kernels  7.42 us (15%)
  local copies, waits for them, and re-layouts  0.64 us (1%)
    ppermute x16, starting transfers between devices, send(): return lax.ppermute(x, ('cells', 'genes'), pairs)  22.2 us
    ppermute x16, waiting for transfers between devices, send(): return lax.ppermute(x, ('cells', 'genes'), pairs)  18.1 us
    pallas_call x1, Pallas kernels, orthonormal(): pl.pallas_call(functools.partial(basis_kernel, scale), out_shape=jax.Shap...  3.24 us
    pallas_call x1, Pallas kernels, log_terms(): pl.pallas_call(functools.partial(log_kernel, width), out_shape=(jax.Shape...  1.92 us
  transfers between devices with their start and end apart: 16, of which 11 were waited for; matrix products, arithmetic and copies ran while one was open for 0% of the time, Pallas kernels for 1%

commit v1 on v0

--- a/solution.py
+++ b/solution.py
@@ -327,8 +327,9 @@
     far, near, own, *blocks = make(me, picks=[4, 2, 0, 3, 1])
     far, near = send(far, 0, 1), send(near, 0, 1)
     near = send(near + send(blocks[0], 1, 1), 2, 1)
-    also = send(blocks[1], 1, 0)
-    far = send(far + lax.optimization_barrier(tree_sum(came)), 4, 1)
+    far = far + lax.optimization_barrier(tree_sum(came))
+    far, last = lax.optimization_barrier((far, blocks[1]))
+    far, also = send(far, 4, 1), send(last, 1, 0)
     return centered_gram([own + also + (near + far)], comps, cell_total)
 
 

time: 48.7 us -> 49.7 us (1.021)
  waiting for transfers between devices: 18.1 us -> 23.5 us
  starting transfers between devices: 22.2 us -> 17.8 us
    ppermute x16, waiting for transfers between devices: 18.1 us -> 23.5 us  [send(): return lax.ppermute(x, ('cells', 'genes'), pairs)]
    ppermute x16, starting transfers between devices: 22.2 us -> 17.8 us  [send(): return lax.ppermute(x, ('cells', 'genes'), pairs)]
where the time goes in v1:
time: 49.7 us; the launch traced here: 49.6 us
  waiting for transfers between devices  23.5 us (47%)
  starting transfers between devices  17.8 us (36%)
  Pallas kernels  7.42 us (15%)
  local copies, waits for them, and re-layouts  0.64 us (1%)
    ppermute x16, waiting for transfers between devices, send(): return lax.ppermute(x, ('cells', 'genes'), pairs)  23.5 us
    ppermute x16, starting transfers between devices, send(): return lax.ppermute(x, ('cells', 'genes'), pairs)  17.8 us
    pallas_call x1, Pallas kernels, orthonormal(): pl.pallas_call(functools.partial(basis_kernel, scale), out_shape=jax.Shap...  3.24 us
    pallas_call x1, Pallas kernels, log_terms(): pl.pallas_call(functools.partial(log_kernel, width), out_shape=(jax.Shape...  1.92 us
  transfers between devices with their start and end apart: 16, of which 11 were waited for; matrix products, arithmetic and copies ran while one was open for 0% of the time, Pallas kernels for 1%

profile of v1, /device:TPU:0, one launch (start us, length us, event | category | flops | bytes accessed | tf_op | source)
XLA Modules:
  0.0 49.6 jit_solution(6944068219988243574)
XLA Ops:
  0.0 1.9 %log_terms.1 = (bf16[128,4096]{1,0:T(8,128)(2,1)S(1)}, bf16[128,4096]{1,0:T(8,128)(2,1)S(1)}, f32[1,4096]{1,0:T(1,128)S(1)}) custom-call(bf16[128,4096]{1,0:T(8,128)(2,1)} %counts_hbm.1), custom_call_target="tpu_custom_call" | custom-call | flops 10485760 | bytes 4194304 | tf_op jit(solution)/shard_map/log_terms/pallas_call | solution.py:65
  1.9 0.6 %copy-done.1 = s32[1,32]{1,0:T(1,128)S(1)} copy-done((s32[1,32]{1,0:T(1,128)S(1)}, s32[1,32]{1,0:T(1,128)}, u32[]{:S(2)}) %copy-start.1) | copy-done | bytes 152
  2.6 0.9 %scores.1 = (f32[64,128]{1,0:T(8,128)S(1)}, f32[1,4096]{1,0:T(1,128)S(1)}) custom-call(s32[1,32]{1,0:T(1,128)S(1)} %copy-done.1, bf16[64,4096]{1,0:T(8,128)(2,1)S(1)} %copy-done, bf16[128,4096]{1,0:T(8,128)(2,1)S(1)} %get-tuple-element.24.high_ref.refs_2_, bf16[128,4096]{1,0:T(8,128)(2,1)S(1)} %get-tuple-element.25.low_ref.refs_3_), custom_call_target="tpu_custom_call" | custom-call | tf_op jit(solution)/shard_map/scores/pallas_call | solution.py:102
  4.0 0.9 %collective-permute-done = f32[64,128]{1,0:T(8,128)S(1)} collective-permute-done((f32[64,128]{1,0:T(8,128)S(1)}, f32[64,128]{1,0:T(8,128)S(1)}, u32[]{:S(2)}, u32[]{:S(2)}) %collective-permute-start) | collective-permute-done | bytes 32800 | tf_op jit(solution)/shard_map/ppermute | solution.py:301
  4.8 2.6 %collective-permute-start.1 = (f32[64,128]{1,0:T(8,128)S(1)}, f32[64,128]{1,0:T(8,128)S(1)}, u32[]{:S(2)}, u32[]{:S(2)}) collective-permute-start(f32[64,128]{1,0:T(8,128)S(1)} %add.36.refs_0_), channel_id=1, source_target_pairs={{0,3},{1,2},{2,1},{3,0},{4,7},{5,6},{6,5},{7,4},{8,11},{9,10},{10,... | collective-permute-start | bytes 98312 | tf_op jit(solution)/shard_map/ppermute | solution.py:301
  7.5 1.6 %collective-permute-done.1.refs_1_ = f32[64,128]{1,0:T(8,128)S(1)} collective-permute-done((f32[64,128]{1,0:T(8,128)S(1)}, f32[64,128]{1,0:T(8,128)S(1)}, u32[]{:S(2)}, u32[]{:S(2)}) %collective-permute-start.1) | collective-permute-done | bytes 32800 | tf_op jit(solution)/shard_map/ppermute | solution.py:301
  9.5 2.9 %collective-permute-start.3 = (f32[264,128]{1,0:T(8,128)S(1)}, f32[264,128]{1,0:T(8,128)S(1)}, u32[]{:S(2)}, u32[]{:S(2)}) collective-permute-start(f32[264,128]{1,0:T(8,128)S(1)} %get-tuple-element.33), channel_id=1, source_target_pairs={{0,13},{1,12},{2,15},{3,14},{4,9},{5,8},{6,11},{7,10},{8,5},{9,4},... | collective-permute-start | bytes 405512 | tf_op jit(solution)/shard_map/ppermute | solution.py:301
  12.9 0.6 %spread.3 = (f32[264,128]{1,0:T(8,128)S(1)}, f32[264,128]{1,0:T(8,128)S(1)}, f32[264,128]{1,0:T(8,128)S(1)}, f32[264,128]{1,0:T(8,128)S(1)}, f32[264,128]{1,0:T(8,128)S(1)}) custom-call(s32[1]{0:T(128)} %bitcast.me_ref, f32[64,128]{1,0:T(8,128)S(1)} %add.36.refs_0_, f32[64,128]{1,0:T(8,128)S(1)} %collective-permute-done.1.refs_1_, ...), custom_call_target="tpu_custom_call" | custom-call | flops 209715200 | bytes 2097152 | tf_op jit(solution)/shard_map/spread/pallas_call | solution.py:152
  14.1 2.2 %collective-permute-done.3 = f32[264,128]{1,0:T(8,128)S(1)} collective-permute-done((f32[264,128]{1,0:T(8,128)S(1)}, f32[264,128]{1,0:T(8,128)S(1)}, u32[]{:S(2)}, u32[]{:S(2)}) %collective-permute-start.3) | collective-permute-done | bytes 135200 | tf_op jit(solution)/shard_map/ppermute | solution.py:301
  16.2 1.8 %collective-permute-start.8 = (f32[264,128]{1,0:T(8,128)S(1)}, f32[264,128]{1,0:T(8,128)S(1)}, u32[]{:S(2)}, u32[]{:S(2)}) collective-permute-start(f32[264,128]{1,0:T(8,128)S(1)} %get-tuple-element.39), channel_id=1, source_target_pairs={{0,5},{1,4},{2,7},{3,6},{4,1},{5,0},{6,3},{7,2},{8,13},{9,12},{10,... | collective-permute-start | bytes 405512 | tf_op jit(solution)/shard_map/ppermute | solution.py:301
  18.0 1.5 %collective-permute-done.4 = f32[264,128]{1,0:T(8,128)S(1)} collective-permute-done((f32[264,128]{1,0:T(8,128)S(1)}, f32[264,128]{1,0:T(8,128)S(1)}, u32[]{:S(2)}, u32[]{:S(2)}) %collective-permute-start.4) | collective-permute-done | bytes 135200 | tf_op jit(solution)/shard_map/ppermute | solution.py:301
  19.6 2.6 %collective-permute-start.10 = (f32[264,128]{1,0:T(8,128)S(1)}, f32[264,128]{1,0:T(8,128)S(1)}, u32[]{:S(2)}, u32[]{:S(2)}) collective-permute-start(f32[264,128]{1,0:T(8,128)S(1)} %add.39), channel_id=1, source_target_pairs={{0,17},{1,16},{2,19},{3,18},{4,21},{5,20},{6,23},{7,22},{8,25},{9,... | collective-permute-start | bytes 405512 | tf_op jit(solution)/shard_map/ppermute | solution.py:301
  22.2 1.4 %collective-permute-start.6 = (f32[264,128]{1,0:T(8,128)S(1)}, f32[264,128]{1,0:T(8,128)S(1)}, u32[]{:S(2)}, u32[]{:S(2)}) collective-permute-start(f32[264,128]{1,0:T(8,128)S(1)} %get-tuple-element.37), channel_id=1, source_target_pairs={{0,4},{1,5},{2,6},{3,7},{4,0},{5,1},{6,2},{7,3},{8,12},{9,13},{10,... | collective-permute-start | bytes 405512 | tf_op jit(solution)/shard_map/ppermute | solution.py:301
  23.7 1.3 %collective-permute-start.9 = (f32[264,128]{1,0:T(8,128)S(1)}, f32[264,128]{1,0:T(8,128)S(1)}, u32[]{:S(2)}, u32[]{:S(2)}) collective-permute-start(f32[264,128]{1,0:T(8,128)S(1)} %add.41), channel_id=1, source_target_pairs={{0,9},{1,8},{2,11},{3,10},{4,13},{5,12},{6,15},{7,14},{8,1},{9,0},... | collective-permute-start | bytes 405512 | tf_op jit(solution)/shard_map/ppermute | solution.py:301
  25.0 4.0 %collective-permute-done.10 = f32[264,128]{1,0:T(8,128)S(1)} collective-permute-done((f32[264,128]{1,0:T(8,128)S(1)}, f32[264,128]{1,0:T(8,128)S(1)}, u32[]{:S(2)}, u32[]{:S(2)}) %collective-permute-start.10) | collective-permute-done | bytes 135200 | tf_op jit(solution)/shard_map/ppermute | solution.py:301
  29.0 2.1 %collective-permute-done.9 = f32[264,128]{1,0:T(8,128)S(1)} collective-permute-done((f32[264,128]{1,0:T(8,128)S(1)}, f32[264,128]{1,0:T(8,128)S(1)}, u32[]{:S(2)}, u32[]{:S(2)}) %collective-permute-start.9) | collective-permute-done | bytes 135200 | tf_op jit(solution)/shard_map/ppermute | solution.py:301
  31.7 1.1 %collective-permute-done.11 = f32[32,128]{1,0:T(8,128)S(1)} collective-permute-done((f32[32,128]{1,0:T(8,128)S(1)}, f32[32,128]{1,0:T(8,128)S(1)}, u32[]{:S(2)}, u32[]{:S(2)}) %collective-permute-start.11) | collective-permute-done | bytes 16416 | tf_op jit(solution)/shard_map/ppermute | solution.py:301
  32.7 1.4 %collective-permute-start.12 = (f32[32,128]{1,0:T(8,128)S(1)}, f32[32,128]{1,0:T(8,128)S(1)}, u32[]{:S(2)}, u32[]{:S(2)}) collective-permute-start(f32[32,128]{1,0:T(8,128)S(1)} %add.44), channel_id=1, source_target_pairs={{0,3},{1,2},{2,1},{3,0},{4,7},{5,6},{6,5},{7,4},{8,11},{9,10},{10,... | collective-permute-start | bytes 49160 | tf_op jit(solution)/shard_map/ppermute | solution.py:301
  34.1 1.8 %collective-permute-done.12 = f32[32,128]{1,0:T(8,128)S(1)} collective-permute-done((f32[32,128]{1,0:T(8,128)S(1)}, f32[32,128]{1,0:T(8,128)S(1)}, u32[]{:S(2)}, u32[]{:S(2)}) %collective-permute-start.12) | collective-permute-done | bytes 16416 | tf_op jit(solution)/shard_map/ppermute | solution.py:301
  36.4 2.7 %collective-permute-done.13 = f32[32,128]{1,0:T(8,128)S(1)} collective-permute-done((f32[32,128]{1,0:T(8,128)S(1)}, f32[32,128]{1,0:T(8,128)S(1)}, u32[]{:S(2)}, u32[]{:S(2)}) %collective-permute-start.13) | collective-permute-done | bytes 16416 | tf_op jit(solution)/shard_map/ppermute | solution.py:301
  39.1 3.2 %collective-permute-done.14 = f32[32,128]{1,0:T(8,128)S(1)} collective-permute-done((f32[32,128]{1,0:T(8,128)S(1)}, f32[32,128]{1,0:T(8,128)S(1)}, u32[]{:S(2)}, u32[]{:S(2)}) %collective-permute-start.14) | collective-permute-done | bytes 16416 | tf_op jit(solution)/shard_map/ppermute | solution.py:301
  42.3 1.4 %collective-permute-start.15 = (f32[32,128]{1,0:T(8,128)S(1)}, f32[32,128]{1,0:T(8,128)S(1)}, u32[]{:S(2)}, u32[]{:S(2)}) collective-permute-start(f32[32,128]{1,0:T(8,128)S(1)} %add.47.refs_0_), channel_id=1, source_target_pairs={{0,17},{1,16},{2,19},{3,18},{4,21},{5,20},{6,23},{7,22},{8,25},{9,... | collective-permute-start | bytes 49160 | tf_op jit(solution)/shard_map/ppermute | solution.py:301
  43.7 2.6 %collective-permute-done.15.refs_1_ = f32[32,128]{1,0:T(8,128)S(1)} collective-permute-done((f32[32,128]{1,0:T(8,128)S(1)}, f32[32,128]{1,0:T(8,128)S(1)}, u32[]{:S(2)}, u32[]{:S(2)}) %collective-permute-start.15) | collective-permute-done | bytes 16416 | tf_op jit(solution)/shard_map/ppermute | solution.py:301
  46.3 3.2 %orthonormal.1 = f32[64,512]{1,0:T(8,128)} custom-call(f32[32,128]{1,0:T(8,128)S(1)} %add.47.refs_0_, f32[32,128]{1,0:T(8,128)S(1)} %collective-permute-done.15.refs_1_, f32[64,512]{1,0:T(8,128)S(1)} %get-tuple-element.42.refs_2_), custom_call_target="tpu_custom_call" | custom-call | tf_op jit(solution)/shard_map/orthonormal/pallas_call | solution.py:285
  (27 shorter events, 3.3 us)
Async XLA Ops:
  0.0 1.9 %copy-start = (bf16[64,4096]{1,0:T(8,128)(2,1)S(1)}, bf16[64,4096]{1,0:T(8,128)(2,1)}, u32[]{:S(2)}) copy-start(bf16[64,4096]{1,0:T(8,128)(2,1)} %basis_ref.1) | copy-start | bytes 1572868
  1.9 0.7 %copy-start.1 = (s32[1,32]{1,0:T(1,128)S(1)}, s32[1,32]{1,0:T(1,128)}, u32[]{:S(2)}) copy-start(s32[1,32]{1,0:T(1,128)} %occ_ref.1) | copy-start | bytes 388
  3.5 1.4 %collective-permute-start = (f32[64,128]{1,0:T(8,128)S(1)}, f32[64,128]{1,0:T(8,128)S(1)}, u32[]{:S(2)}, u32[]{:S(2)}) collective-permute-start(f32[64,128]{1,0:T(8,128)S(1)} %get-tuple-element.26), channel_id=1, source_target_pairs={{0,1},{1,0},{2,3},{3,2},{4,5},{5,4},{6,7},{7,6},{8,9},{9,8},{10,11... | collective-permute-start | bytes 98312 | tf_op jit(solution)/shard_map/ppermute | solution.py:301
  4.8 4.2 %collective-permute-start.1 = (f32[64,128]{1,0:T(8,128)S(1)}, f32[64,128]{1,0:T(8,128)S(1)}, u32[]{:S(2)}, u32[]{:S(2)}) collective-permute-start(f32[64,128]{1,0:T(8,128)S(1)} %add.36.refs_0_), channel_id=1, source_target_pairs={{0,3},{1,2},{2,1},{3,0},{4,7},{5,6},{6,5},{7,4},{8,11},{9,10},{10,... | collective-permute-start | bytes 98312 | tf_op jit(solution)/shard_map/ppermute | solution.py:301
  9.5 6.8 %collective-permute-start.3 = (f32[264,128]{1,0:T(8,128)S(1)}, f32[264,128]{1,0:T(8,128)S(1)}, u32[]{:S(2)}, u32[]{:S(2)}) collective-permute-start(f32[264,128]{1,0:T(8,128)S(1)} %get-tuple-element.33), channel_id=1, source_target_pairs={{0,13},{1,12},{2,15},{3,14},{4,9},{5,8},{6,11},{7,10},{8,5},{9,4},... | collective-permute-start | bytes 405512 | tf_op jit(solution)/shard_map/ppermute | solution.py:301
  12.3 7.2 %collective-permute-start.4 = (f32[264,128]{1,0:T(8,128)S(1)}, f32[264,128]{1,0:T(8,128)S(1)}, u32[]{:S(2)}, u32[]{:S(2)}) collective-permute-start(f32[264,128]{1,0:T(8,128)S(1)} %get-tuple-element.34), channel_id=1, source_target_pairs={{0,9},{1,8},{2,11},{3,10},{4,13},{5,12},{6,15},{7,14},{8,1},{9,0},... | collective-permute-start | bytes 405512 | tf_op jit(solution)/shard_map/ppermute | solution.py:301
  12.7 6.8 %collective-permute-start.5 = (f32[264,128]{1,0:T(8,128)S(1)}, f32[264,128]{1,0:T(8,128)S(1)}, u32[]{:S(2)}, u32[]{:S(2)}) collective-permute-start(f32[264,128]{1,0:T(8,128)S(1)} %get-tuple-element.35), channel_id=1, source_target_pairs={{0,5},{1,4},{2,7},{3,6},{4,1},{5,0},{6,3},{7,2},{8,13},{9,12},{10,... | collective-permute-start | bytes 405512 | tf_op jit(solution)/shard_map/ppermute | solution.py:301
  13.5 6.1 %collective-permute-start.2 = (f32[264,128]{1,0:T(8,128)S(1)}, f32[264,128]{1,0:T(8,128)S(1)}, u32[]{:S(2)}, u32[]{:S(2)}) collective-permute-start(f32[264,128]{1,0:T(8,128)S(1)} %get-tuple-element.32), channel_id=1, source_target_pairs={{0,1},{1,0},{2,3},{3,2},{4,5},{5,4},{6,7},{7,6},{8,9},{9,8},{10,11... | collective-permute-start | bytes 405512 | tf_op jit(solution)/shard_map/ppermute | solution.py:301
  13.7 10.0 %collective-permute-start.7 = (f32[264,128]{1,0:T(8,128)S(1)}, f32[264,128]{1,0:T(8,128)S(1)}, u32[]{:S(2)}, u32[]{:S(2)}) collective-permute-start(f32[264,128]{1,0:T(8,128)S(1)} %get-tuple-element.38), channel_id=1, source_target_pairs={{0,1},{1,0},{2,3},{3,2},{4,5},{5,4},{6,7},{7,6},{8,9},{9,8},{10,11... | collective-permute-start | bytes 405512 | tf_op jit(solution)/shard_map/ppermute | solution.py:301
  16.2 7.4 %collective-permute-start.8 = (f32[264,128]{1,0:T(8,128)S(1)}, f32[264,128]{1,0:T(8,128)S(1)}, u32[]{:S(2)}, u32[]{:S(2)}) collective-permute-start(f32[264,128]{1,0:T(8,128)S(1)} %get-tuple-element.39), channel_id=1, source_target_pairs={{0,5},{1,4},{2,7},{3,6},{4,1},{5,0},{6,3},{7,2},{8,13},{9,12},{10,... | collective-permute-start | bytes 405512 | tf_op jit(solution)/shard_map/ppermute | solution.py:301
  19.6 9.4 %collective-permute-start.10 = (f32[264,128]{1,0:T(8,128)S(1)}, f32[264,128]{1,0:T(8,128)S(1)}, u32[]{:S(2)}, u32[]{:S(2)}) collective-permute-start(f32[264,128]{1,0:T(8,128)S(1)} %add.39), channel_id=1, source_target_pairs={{0,17},{1,16},{2,19},{3,18},{4,21},{5,20},{6,23},{7,22},{8,25},{9,... | collective-permute-start | bytes 405512 | tf_op jit(solution)/shard_map/ppermute | solution.py:301
  22.2 6.8 %collective-permute-start.6 = (f32[264,128]{1,0:T(8,128)S(1)}, f32[264,128]{1,0:T(8,128)S(1)}, u32[]{:S(2)}, u32[]{:S(2)}) collective-permute-start(f32[264,128]{1,0:T(8,128)S(1)} %get-tuple-element.37), channel_id=1, source_target_pairs={{0,4},{1,5},{2,6},{3,7},{4,0},{5,1},{6,2},{7,3},{8,12},{9,13},{10,... | collective-permute-start | bytes 405512 | tf_op jit(solution)/shard_map/ppermute | solution.py:301
  23.7 7.4 %collective-permute-start.9 = (f32[264,128]{1,0:T(8,128)S(1)}, f32[264,128]{1,0:T(8,128)S(1)}, u32[]{:S(2)}, u32[]{:S(2)}) collective-permute-start(f32[264,128]{1,0:T(8,128)S(1)} %add.41), channel_id=1, source_target_pairs={{0,9},{1,8},{2,11},{3,10},{4,13},{5,12},{6,15},{7,14},{8,1},{9,0},... | collective-permute-start | bytes 405512 | tf_op jit(solution)/shard_map/ppermute | solution.py:301
  31.5 1.2 %collective-permute-start.11 = (f32[32,128]{1,0:T(8,128)S(1)}, f32[32,128]{1,0:T(8,128)S(1)}, u32[]{:S(2)}, u32[]{:S(2)}) collective-permute-start(f32[32,128]{1,0:T(8,128)S(1)} %get-tuple-element.41), channel_id=1, source_target_pairs={{0,1},{1,0},{2,3},{3,2},{4,5},{5,4},{6,7},{7,6},{8,9},{9,8},{10,11... | collective-permute-start | bytes 49160 | tf_op jit(solution)/shard_map/ppermute | solution.py:301
  32.7 3.2 %collective-permute-start.12 = (f32[32,128]{1,0:T(8,128)S(1)}, f32[32,128]{1,0:T(8,128)S(1)}, u32[]{:S(2)}, u32[]{:S(2)}) collective-permute-start(f32[32,128]{1,0:T(8,128)S(1)} %add.44), channel_id=1, source_target_pairs={{0,3},{1,2},{2,1},{3,0},{4,7},{5,6},{6,5},{7,4},{8,11},{9,10},{10,... | collective-permute-start | bytes 49160 | tf_op jit(solution)/shard_map/ppermute | solution.py:301
  35.9 3.2 %collective-permute-start.13 = (f32[32,128]{1,0:T(8,128)S(1)}, f32[32,128]{1,0:T(8,128)S(1)}, u32[]{:S(2)}, u32[]{:S(2)}) collective-permute-start(f32[32,128]{1,0:T(8,128)S(1)} %add.45), channel_id=1, source_target_pairs={{0,5},{1,4},{2,7},{3,6},{4,1},{5,0},{6,3},{7,2},{8,13},{9,12},{10,... | collective-permute-start | bytes 49160 | tf_op jit(solution)/shard_map/ppermute | solution.py:301
  39.1 3.2 %collective-permute-start.14 = (f32[32,128]{1,0:T(8,128)S(1)}, f32[32,128]{1,0:T(8,128)S(1)}, u32[]{:S(2)}, u32[]{:S(2)}) collective-permute-start(f32[32,128]{1,0:T(8,128)S(1)} %add.46), channel_id=1, source_target_pairs={{0,9},{1,8},{2,11},{3,10},{4,13},{5,12},{6,15},{7,14},{8,1},{9,0},... | collective-permute-start | bytes 49160 | tf_op jit(solution)/shard_map/ppermute | solution.py:301
  42.3 4.1 %collective-permute-start.15 = (f32[32,128]{1,0:T(8,128)S(1)}, f32[32,128]{1,0:T(8,128)S(1)}, u32[]{:S(2)}, u32[]{:S(2)}) collective-permute-start(f32[32,128]{1,0:T(8,128)S(1)} %add.47.refs_0_), channel_id=1, source_target_pairs={{0,17},{1,16},{2,19},{3,18},{4,21},{5,20},{6,23},{7,22},{8,25},{9,... | collective-permute-start | bytes 49160 | tf_op jit(solution)/shard_map/ppermute | solution.py:301
